TPU v7x, 128 devices: a whole 4x4x4 slice. The times are simulated.
128 devices in a mesh: dp: 4 (over x), seq: 16 (over z, y), tensor: 2 (over core).
Axes of the slice: x: 4, y: 4, z: 4, core: 2. Of those that a mesh axis runs over, the one named last changes fastest.
Arguments:
- queries: bfloat16 [8192, 4096], P(('dp', 'seq'), 'tensor'), may hold values from -6 to 6
- keys: bfloat16 [8192, 512], P(('dp', 'seq'), 'tensor'), may hold values from -6 to 6
- values: bfloat16 [8192, 512], P(('dp', 'seq'), 'tensor'), may hold values from -6 to 6
- out_weight: bfloat16 [4096, 8192], P('tensor', 'seq'), may hold values from -0.09375 to 0.09375
- doc_len: int32 [4, 16], P('dp'), may hold values from 1 to 1024, as said below
- destination: int32 [4, 16], P('dp'), may hold values from 0 to 3, as said below
Outputs:
- attended: bfloat16 [16384, 8192], P(('dp', 'tensor'), 'seq')
Inputs may be any that keep to these rules, and one draw needn't show every extreme that they name: `doc_len`: each row sums to 2048; in each row one document has exactly 1024 tokens. destination[g, j] is g or g XOR (2).
All inputs are finite; a program needn't handle non-finite values.
Results may differ from a plain program's by a relative error of at most 0.0095.
Values may be sent and summed in bfloat16 or wider, within the bound.
A program may use at most 192 MiB of HBM per device.

v0:
```python
import math

import jax
import jax.numpy as jnp
from jax import lax
from jax.sharding import PartitionSpec as P

QUERY_HEADS = 32
KEY_VALUE_HEADS = 4
HEAD_SIZE = 128


NEG = -1e30


def from_partner(block, axis, bit):
    count = lax.axis_size(axis)
    route = []
    for low in range(count):
        high = low | 1 << bit
        if high != low and high < count:
            route += [(low, high), (high, low)]
    return lax.ppermute(block, axis, route)


def visible_mask(passage_probe_vector, pos_query, doc_key, pos_key):
    same = passage_probe_vector[:, None] == doc_key[None, :]
    before = pos_key[None, :] <= pos_query[:, None]
    return same & before & (doc_key[None, :] >= 0)


def block_scores(query_block, key_block, scale):
    return (
        jnp.einsum("qd,kd->qk", query_block, key_block, preferred_element_type=jnp.float32) * scale
    )


def attend_all(query_head, key_head, value_head, doc_q, pos_q, doc_k, pos_k, width):
    rows = query_head.shape[0]
    scale = 1.0 / math.sqrt(query_head.shape[1])

    def one_block(index):
        start = index * width
        query_block = lax.dynamic_slice_in_dim(query_head, start, width, 0)
        passage_probe_vector = lax.dynamic_slice_in_dim(doc_q, start, width, 0)
        pos_query = lax.dynamic_slice_in_dim(pos_q, start, width, 0)
        scores = block_scores(query_block, key_head, scale)
        scores = jnp.where(visible_mask(passage_probe_vector, pos_query, doc_k, pos_k), scores, NEG)
        top = jnp.max(scores, axis=1, keepdims=True)
        expo = jnp.exp(scores - top)
        total = jnp.sum(expo, axis=1, keepdims=True)
        weights = (expo / total).astype(jnp.bfloat16)
        blended_outputs = jnp.dot(weights, value_head, preferred_element_type=jnp.float32)
        active_indicator = (passage_probe_vector >= 0).astype(jnp.float32)[:, None]
        return (blended_outputs * active_indicator).astype(jnp.bfloat16)

    blocks = lax.map(one_block, jnp.arange(rows // width, dtype=jnp.int32))
    return blocks.reshape(rows, value_head.shape[1])


def attend_heads(query_rows, first_head, group_k, group_v, doc_q, pos_q, doc_k, pos_k):
    ratio_value = QUERY_HEADS // KEY_VALUE_HEADS
    width = min(512, query_rows.shape[0])
    kv_index = (first_head + 0) // ratio_value
    key_head = lax.dynamic_slice_in_dim(group_k, kv_index * HEAD_SIZE, HEAD_SIZE, 1)
    value_head = lax.dynamic_slice_in_dim(group_v, kv_index * HEAD_SIZE, HEAD_SIZE, 1)
    pieces = attend_all(query_rows, key_head, value_head, doc_q, pos_q, doc_k, pos_k, width)
    return pieces


def reduce_groups(total):
    return lax.psum_scatter(
        total.astype(jnp.bfloat16), "tensor", scatter_dimension=0, tiled=True
    ).astype(jnp.float32)


def shards(queries, keys, values, out_weight, doc_len, destination):
    tok = queries.shape[0]
    grp = lax.axis_index("dp")
    shard = lax.axis_index("seq")
    lengths = doc_len[0]
    docs = lengths.shape[0]
    ends = jnp.cumsum(lengths)
    starts = ends - lengths
    place = shard * tok + jnp.arange(tok, dtype=jnp.int32)
    doc_index = jnp.sum((ends[None, :] <= place[:, None]).astype(jnp.int32), axis=1)
    onehot = (doc_index[:, None] == jnp.arange(docs, dtype=jnp.int32)[None, :]).astype(jnp.int32)
    position = place - jnp.sum(onehot * starts[None, :], axis=1)
    target = jnp.sum(onehot * destination[0][None, :], axis=1)
    doc_id = grp * docs + doc_index
    labels = jnp.stack([doc_id, position, target], axis=0)
    partner_bit = lax.axis_size("dp").bit_length() - 2
    far_q, far_k, far_v, far_labels = from_partner(
        (queries, keys, values, labels), "dp", partner_bit
    )
    slot_q = jnp.concatenate([queries, far_q], axis=0)
    slot_k = jnp.concatenate([keys, far_k], axis=0)
    slot_v = jnp.concatenate([values, far_v], axis=0)
    slot_labels = jnp.concatenate([labels, far_labels], axis=1)
    active_slot_items = slot_labels[2] == grp
    slot_doc = jnp.where(active_slot_items, slot_labels[0], -1)
    slot_info = jnp.stack([slot_doc, slot_labels[1]], axis=0).astype(jnp.int32)
    group_k, group_v, group_info = (
        lax.all_gather(slot_k, "seq", axis=0, tiled=True),
        lax.all_gather(slot_v, "seq", axis=0, tiled=True),
        lax.all_gather(slot_info, "seq", axis=1, tiled=True),
    )
    group_doc = group_info[0]
    group_pos = group_info[1]
    head_q = lax.all_to_all(slot_q, "seq", split_axis=1, concat_axis=0, tiled=True)
    heads_here = head_q.shape[1] // HEAD_SIZE
    heads_out = attend_heads(
        head_q, shard * heads_here, group_k, group_v, group_doc, group_pos, group_doc, group_pos
    )
    total = jnp.dot(
        lax.all_gather(heads_out, "seq", axis=1, tiled=True),
        out_weight,
        preferred_element_type=jnp.float32,
    )
    summed = reduce_groups(total)
    return summed.astype(jnp.bfloat16)


def solution(mesh):
    in_specs = (
        P(("dp", "seq"), "tensor"),
        P(("dp", "seq"), "tensor"),
        P(("dp", "seq"), "tensor"),
        P("tensor", "seq"),
        P("dp", None),
        P("dp", None),
    )
    out_specs = P(("dp", "tensor"), "seq")
    return jax.shard_map(shards, mesh=mesh, in_specs=in_specs, out_specs=out_specs, check_vma=False)
```

profile of v0, /device:TPU:1, one launch (start us, length us, event | category | flops | bytes accessed | tf_op | source)
XLA Modules:
  0.0 342.3 jit_solution(10781828779736432021)
XLA Ops:
  6.5 3.6 %collective-permute-start.2 = (bf16[128,256]{1,0:T(8,128)(2,1)}, bf16[128,256]{1,0:T(8,128)(2,1)S(1)}, u32[]{:S(2)}, u32[]{:S(2)}) collective-permute-start(bf16[128,256]{1,0:T(8,128)(2,1)} %param.9), channel_id=1, source_target_pairs={{0,64},{64,0},{32,96},{96,32},{1,65},{65,1},{33,97},{97,33},{2,66}... | collective-permute-start | bytes 196616 | tf_op jit(solution)/shard_map/ppermute | solution.py:23
  13.6 3.0 collective-permute-start.3
  20.0 3.0 collective-permute-start.1
  25.6 6.6 %collective-permute-done = s32[3,128]{1,0:T(4,128)S(1)} collective-permute-done((s32[3,128]{1,0:T(4,128)S(1)}, s32[3,128]{1,0:T(4,128)S(1)}, u32[]{:S(2)}, u32[]{:S(2)}) %collective-permute-start) | collective-permute-done | bytes 1568 | tf_op jit(solution)/shard_map/ppermute | solution.py:23
  32.2 20.9 %all_gather.12 = s32[2,4096]{1,0:T(2,128)S(1)} all-gather(s32[2,256]{1,0:T(2,128)S(1)} %pad_add_fusion.1), channel_id=1, replica_groups=mesh['dp'=4,'seq'=16,'tensor'=2] {'seq'}, dimensions={1}, use_global_device_ids=true | all-gather | bytes 34816 | tf_op jit(solution)/shard_map/all_gather | solution.py:106
  55.4 4.3 %all-to-all-start = ((bf16[256,16,128]{2,0,1:T(8,128)(2,1)}), bf16[256,16,128]{2,0,1:T(8,128)(2,1)}, u32[]{:S(2)}, u32[]{:S(2)}) async-start(bf16[256,16,128]{2,0,1:T(8,128)(2,1)} %copy_bitcast_fusion), calls=%async_computation | async-start | bytes 2097152 | tf_op jit(solution)/shard_map/all_to_all | solution.py:110
  63.0 46.6 %all-gather.6.cloned.1.call-done = bf16[4096,256]{1,0:T(8,128)(2,1)} async-done(((bf16[256,256]{1,0:T(8,128)(2,1)}), bf16[4096,256]{1,0:T(8,128)(2,1)}) %all-gather.6.cloned.1.call-update) | async-done | bytes 2097168 | tf_op jit(solution)/shard_map/all_gather | solution.py:105
  111.9 74.0 %while.10 = (s32[]{:T(128)}, bf16[8,512,128]{2,1,0:T(8,128)(2,1)}, s32[8]{0:T(128)S(1)}, s32[4096]{0:T(1024)S(1)}, s32[1,4096]{1,0:T(1,128)S(1)}, /*index=5*/s32...) while((s32[]{:T(128)}, bf16[8,512,128]{2,1,0:T(8,128)(2,1)}, ...), condition=%wide.region_7.8_spmd, body=%wide.region_4.7_spmd.sunk | while | flops 1099042816 | bytes 31803636 | solution.py:57
  113.2 3.7 %fusion.22 = (f32[512]{0:T(512)S(1)}, f32[512,4096]{1,0:T(8,128)S(1)}) fusion(bf16[4096,128]{1,0:T(8,128)(2,1)S(1)} %get-tuple-element.193, bf16[4096,128]{1,0:T(8,128)(2,1)} %get-tuple-element.192, s32[]{:T(128)S(6)} %select_n.29, pred[4096]{0:T(1024)(128)(4,1)S(1)} %broadcast_compare_fusion.2, s32[512]{0:T(512)S(1)} %dynamic_slice.35, ...), kind=kOutput, calls=%fused_computation.35.clone.1 | convolution fusion | flops 551550464 | bytes 9611268 | tf_op jit(solution)/shard_map/while/body/eval_jaxpr/qd,kd->qk/dot_general | solution.py:34
  118.2 2.9 fusion.24
  122.4 3.7 %fusion.22 = (f32[512]{0:T(512)S(1)}, f32[512,4096]{1,0:T(8,128)S(1)}) fusion(bf16[4096,128]{1,0:T(8,128)(2,1)S(1)} %get-tuple-element.193, bf16[4096,128]{1,0:T(8,128)(2,1)} %get-tuple-element.192, s32[]{:T(128)S(6)} %select_n.29, pred[4096]{0:T(1024)(128)(4,1)S(1)} %broadcast_compare_fusion.2, s32[512]{0:T(512)S(1)} %dynamic_slice.35, ...), kind=kOutput, calls=%fused_computation.35.clone.1 | convolution fusion | flops 551550464 | bytes 9611268 | tf_op jit(solution)/shard_map/while/body/eval_jaxpr/qd,kd->qk/dot_general | solution.py:34
  127.5 2.9 fusion.24
  131.7 3.7 %fusion.22 = (f32[512]{0:T(512)S(1)}, f32[512,4096]{1,0:T(8,128)S(1)}) fusion(bf16[4096,128]{1,0:T(8,128)(2,1)S(1)} %get-tuple-element.193, bf16[4096,128]{1,0:T(8,128)(2,1)} %get-tuple-element.192, s32[]{:T(128)S(6)} %select_n.29, pred[4096]{0:T(1024)(128)(4,1)S(1)} %broadcast_compare_fusion.2, s32[512]{0:T(512)S(1)} %dynamic_slice.35, ...), kind=kOutput, calls=%fused_computation.35.clone.1 | convolution fusion | flops 551550464 | bytes 9611268 | tf_op jit(solution)/shard_map/while/body/eval_jaxpr/qd,kd->qk/dot_general | solution.py:34
  136.7 2.9 fusion.24
  140.9 3.7 %fusion.22 = (f32[512]{0:T(512)S(1)}, f32[512,4096]{1,0:T(8,128)S(1)}) fusion(bf16[4096,128]{1,0:T(8,128)(2,1)S(1)} %get-tuple-element.193, bf16[4096,128]{1,0:T(8,128)(2,1)} %get-tuple-element.192, s32[]{:T(128)S(6)} %select_n.29, pred[4096]{0:T(1024)(128)(4,1)S(1)} %broadcast_compare_fusion.2, s32[512]{0:T(512)S(1)} %dynamic_slice.35, ...), kind=kOutput, calls=%fused_computation.35.clone.1 | convolution fusion | flops 551550464 | bytes 9611268 | tf_op jit(solution)/shard_map/while/body/eval_jaxpr/qd,kd->qk/dot_general | solution.py:34
  150.2 3.7 %fusion.22 = (f32[512]{0:T(512)S(1)}, f32[512,4096]{1,0:T(8,128)S(1)}) fusion(bf16[4096,128]{1,0:T(8,128)(2,1)S(1)} %get-tuple-element.193, bf16[4096,128]{1,0:T(8,128)(2,1)} %get-tuple-element.192, s32[]{:T(128)S(6)} %select_n.29, pred[4096]{0:T(1024)(128)(4,1)S(1)} %broadcast_compare_fusion.2, s32[512]{0:T(512)S(1)} %dynamic_slice.35, ...), kind=kOutput, calls=%fused_computation.35.clone.1 | convolution fusion | flops 551550464 | bytes 9611268 | tf_op jit(solution)/shard_map/while/body/eval_jaxpr/qd,kd->qk/dot_general | solution.py:34
  155.2 2.9 fusion.24
  159.4 3.7 %fusion.22 = (f32[512]{0:T(512)S(1)}, f32[512,4096]{1,0:T(8,128)S(1)}) fusion(bf16[4096,128]{1,0:T(8,128)(2,1)S(1)} %get-tuple-element.193, bf16[4096,128]{1,0:T(8,128)(2,1)} %get-tuple-element.192, s32[]{:T(128)S(6)} %select_n.29, pred[4096]{0:T(1024)(128)(4,1)S(1)} %broadcast_compare_fusion.2, s32[512]{0:T(512)S(1)} %dynamic_slice.35, ...), kind=kOutput, calls=%fused_computation.35.clone.1 | convolution fusion | flops 551550464 | bytes 9611268 | tf_op jit(solution)/shard_map/while/body/eval_jaxpr/qd,kd->qk/dot_general | solution.py:34
  168.7 3.7 %fusion.22 = (f32[512]{0:T(512)S(1)}, f32[512,4096]{1,0:T(8,128)S(1)}) fusion(bf16[4096,128]{1,0:T(8,128)(2,1)S(1)} %get-tuple-element.193, bf16[4096,128]{1,0:T(8,128)(2,1)} %get-tuple-element.192, s32[]{:T(128)S(6)} %select_n.29, pred[4096]{0:T(1024)(128)(4,1)S(1)} %broadcast_compare_fusion.2, s32[512]{0:T(512)S(1)} %dynamic_slice.35, ...), kind=kOutput, calls=%fused_computation.35.clone.1 | convolution fusion | flops 551550464 | bytes 9611268 | tf_op jit(solution)/shard_map/while/body/eval_jaxpr/qd,kd->qk/dot_general | solution.py:34
  173.7 2.9 fusion.24
  177.9 3.7 %fusion.22 = (f32[512]{0:T(512)S(1)}, f32[512,4096]{1,0:T(8,128)S(1)}) fusion(bf16[4096,128]{1,0:T(8,128)(2,1)S(1)} %get-tuple-element.193, bf16[4096,128]{1,0:T(8,128)(2,1)} %get-tuple-element.192, s32[]{:T(128)S(6)} %select_n.29, pred[4096]{0:T(1024)(128)(4,1)S(1)} %broadcast_compare_fusion.2, s32[512]{0:T(512)S(1)} %dynamic_slice.35, ...), kind=kOutput, calls=%fused_computation.35.clone.1 | convolution fusion | flops 551550464 | bytes 9611268 | tf_op jit(solution)/shard_map/while/body/eval_jaxpr/qd,kd->qk/dot_general | solution.py:34
  185.9 120.7 %all-gather.8.cloned.1.call-done = bf16[4096,2048]{1,0:T(8,128)(2,1)} async-done(((bf16[4096,128]{1,0:T(8,128)(2,1)}), bf16[4096,2048]{1,0:T(8,128)(2,1)}) %all-gather.8.cloned.1.call-update) | async-done | bytes 16777232 | tf_op jit(solution)/shard_map/all_gather | solution.py:116
  306.6 13.7 %convolution_convert_fusion = bf16[4096,512]{1,0:T(8,128)(2,1)} fusion(bf16[4096,2048]{1,0:T(8,128)(2,1)} %all-gather.8.cloned.1.call-done, bf16[2048,512]{1,0:T(8,128)(2,1)S(1)} %copy-done), kind=kOutput, calls=%fused_computation.13 | convolution fusion | flops 8592031744 | bytes 23068672 | tf_op jit(solution)/shard_map/dot_general | solution.py:115
  320.4 15.4 %reduce-scatter.2.cloned.1.call-done = bf16[2048,512]{1,0:T(8,128)(2,1)} async-done(((bf16[4096,512]{1,0:T(8,128)(2,1)}), bf16[2048,512]{1,0:T(8,128)(2,1)}) %reduce-scatter.2.cloned.1.call-update) | async-done | bytes 2097168 | tf_op jit(solution)/shard_map/reduce_scatter | solution.py:72
  (95 shorter events, 42.2 us)
Async XLA Ops:
  6.5 300.1 %copy-start = (bf16[2048,512]{1,0:T(8,128)(2,1)S(1)}, bf16[2048,512]{1,0:T(8,128)(2,1)}, u32[]{:S(2)}) copy-start(bf16[2048,512]{1,0:T(8,128)(2,1)} %param.11) | copy-start | bytes 6291460
  6.5 55.2 %all-gather.4.cloned.1.call-start = ((), (), s32[]{:S(2)}) async-start(), calls=%async_computation.2 | async-start | bytes 2228224 | tf_op jit(solution)/shard_map/all_gather | solution.py:104
  6.5 5.4 %collective-permute-start.2 = (bf16[128,256]{1,0:T(8,128)(2,1)}, bf16[128,256]{1,0:T(8,128)(2,1)S(1)}, u32[]{:S(2)}, u32[]{:S(2)}) collective-permute-start(bf16[128,256]{1,0:T(8,128)(2,1)} %param.9), channel_id=1, source_target_pairs={{0,64},{64,0},{32,96},{96,32},{1,65},{65,1},{33,97},{97,33},{2,66}... | collective-permute-start | bytes 196616 | tf_op jit(solution)/shard_map/ppermute | solution.py:23
  13.5 96.1 %all-gather.6.cloned.1.call-start = ((), (), s32[]{:S(2)}) async-start(), calls=%async_computation.3 | async-start | bytes 2228224 | tf_op jit(solution)/shard_map/all_gather | solution.py:105
  13.6 4.9 %collective-permute-start.3 = (bf16[128,256]{1,0:T(8,128)(2,1)}, bf16[128,256]{1,0:T(8,128)(2,1)S(1)}, u32[]{:S(2)}, u32[]{:S(2)}) collective-permute-start(bf16[128,256]{1,0:T(8,128)(2,1)} %param.10), channel_id=1, source_target_pairs={{0,64},{64,0},{32,96},{96,32},{1,65},{65,1},{33,97},{97,33},{2,66}... | collective-permute-start | bytes 196616 | tf_op jit(solution)/shard_map/ppermute | solution.py:23
  20.0 33.0 %collective-permute-start.1 = (bf16[128,2048]{1,0:T(8,128)(2,1)}, bf16[128,2048]{1,0:T(8,128)(2,1)S(1)}, u32[]{:S(2)}, u32[]{:S(2)}) collective-permute-start(bf16[128,2048]{1,0:T(8,128)(2,1)} %param.8), channel_id=1, source_target_pairs={{0,64},{64,0},{32,96},{96,32},{1,65},{65,1},{33,97},{97,33},{2,66}... | collective-permute-start | bytes 1572872 | tf_op jit(solution)/shard_map/ppermute | solution.py:23
  25.5 6.7 %collective-permute-start = (s32[3,128]{1,0:T(4,128)S(1)}, s32[3,128]{1,0:T(4,128)S(1)}, u32[]{:S(2)}, u32[]{:S(2)}) collective-permute-start(s32[3,128]{1,0:T(4,128)S(1)} %pad_add_fusion), channel_id=1, source_target_pairs={{0,64},{64,0},{32,96},{96,32},{1,65},{65,1},{33,97},{97,33},{2,66}... | collective-permute-start | bytes 4616 | tf_op jit(solution)/shard_map/ppermute | solution.py:23
  55.4 56.5 %all-to-all-start = ((bf16[256,16,128]{2,0,1:T(8,128)(2,1)}), bf16[256,16,128]{2,0,1:T(8,128)(2,1)}, u32[]{:S(2)}, u32[]{:S(2)}) async-start(bf16[256,16,128]{2,0,1:T(8,128)(2,1)} %copy_bitcast_fusion), calls=%async_computation | async-start | bytes 2097152 | tf_op jit(solution)/shard_map/all_to_all | solution.py:110
  59.7 246.9 %all-gather.8.cloned.1.call-start = ((), (), s32[]{:S(2)}) async-start(), calls=%async_computation.4 | async-start | bytes 17825792 | tf_op jit(solution)/shard_map/all_gather | solution.py:116
  116.9 1.3 copy-start.1
  126.2 1.3 copy-start.1
  135.4 1.3 copy-start.1
  144.7 1.3 copy-start.1
  153.9 1.3 copy-start.1
  163.2 1.3 copy-start.1
  172.4 1.3 copy-start.1
  181.7 1.3 copy-start.1
  185.9 149.9 %reduce-scatter.2.cloned.1.call-start = ((), (), s32[]{:S(2)}) async-start(), calls=%async_computation.5 | async-start | bytes 6291456 | tf_op jit(solution)/shard_map/reduce_scatter | solution.py:72
Sparse Core Ops, SparseCore 0:
  13.6 48.0 all-gather.3
  63.8 45.6 all-gather.5
  186.0 120.5 all-gather.7
  320.5 15.1 reduce-scatter.1
where the time goes:
time: 343 us; the launch traced here: 342 us
  waiting for transfers between devices  195 us (57%)
  matrix products  66.7 us (19%)
  blocking collectives  20.9 us (6%)
  other arithmetic  17.9 us (5%)
  starting transfers between devices  14.2 us (4%)
  between operations  13.2 us (4%)
  local copies, waits for them, and re-layouts  9.7 us (3%)
  loops' own time  4.78 us (1%)
    all_gather x1, waiting for transfers between devices, shards(): lax.all_gather(heads_out, 'seq', axis=1, tiled=True)  121 us
    all_gather x1, waiting for transfers between devices, shards(): lax.all_gather(slot_v, 'seq', axis=0, tiled=True)  46.6 us
    dot_general x8, matrix products, block_scores(): jnp.einsum('qd,kd->qk', query_block, key_block, preferred_element_type=jn...  29.8 us
    dot_general x8, matrix products, one_block(): jnp.dot(weights, value_head, preferred_element_type=jnp.float32)  23.1 us
    all_gather x1, blocking collectives, shards(): lax.all_gather(slot_info, 'seq', axis=1, tiled=True)  20.9 us
    reduce_scatter x1, waiting for transfers between devices, reduce_groups(): lax.psum_scatter(total.astype(jnp.bfloat16), 'tensor', scatter_dimension=...  15.4 us
    dot_general x1, matrix products, shards(): jnp.dot(lax.all_gather(heads_out, 'seq', axis=1, tiled=True), out_weight,...  13.7 us
    ppermute x4, waiting for transfers between devices, from_partner(): return lax.ppermute(block, axis, route)  10.3 us
  transfers between devices with their start and end apart: 9, of which 7 were waited for; matrix products, arithmetic and copies ran while one was open for 3% of the time, Pallas kernels for 0%

commit v1 on v0

v1 whole, which is shorter than its diff:
```python
import math

import jax
import jax.numpy as jnp
from jax import lax
from jax.experimental import pallas as pl
from jax.experimental.pallas import tpu as pltpu
from jax.sharding import PartitionSpec as P

MESH = pl.DeviceIdType.MESH
HEAD = 128
TOK = 128
DOCS = 16
WINDOW = 9
HALF = TOK // 2
PIECE = TOK // 4
BF16 = jnp.bfloat16
F32 = jnp.float32
NEG = -1e30


def kernel(
    q_hbm, k_hbm, v_hbm, w_hbm, len_ref, dest_ref, out_hbm,
    q_ref, w_ref, kv, gathered, bias, mine, to_pair, from_pair, far, result,
    in_sems, kv_send, kv_recv, g_send, g_recv, p_send, p_recv, x_send, x_recv, out_sem,
):
    x = lax.axis_index("dp")
    s = lax.axis_index("seq")
    t = lax.axis_index("tensor")
    z = s // 4
    y = s % 4

    def at(zz, yy):
        return (x, (zz % 4) * 4 + yy % 4, t)

    pair = (x, s, 1 - t)
    across = ((x + 2) % 4, s, t)

    in_copies = [
        pltpu.make_async_copy(k_hbm, kv.at[WINDOW - 1, :, pl.ds(0, 256)], in_sems.at[0]),
        pltpu.make_async_copy(v_hbm, kv.at[WINDOW - 1, :, pl.ds(256, 256)], in_sems.at[1]),
        pltpu.make_async_copy(q_hbm, q_ref, in_sems.at[2]),
        pltpu.make_async_copy(w_hbm, w_ref, in_sems.at[3]),
    ]
    for copy in in_copies:
        copy.start()

    barrier = pltpu.get_barrier_semaphore()
    others = [at(z, y + 1), at(z, y + 2), at(z, y + 3), at(z + 1, y), at(z + 2, y), at(z + 3, y), pair, across]
    for other in others:
        pl.semaphore_signal(barrier, inc=1, device_id=other, device_id_type=MESH)
    pl.semaphore_wait(barrier, len(others))

    def kv_copy(src, dst, index, device):
        return pltpu.make_async_remote_copy(
            src_ref=kv.at[src], dst_ref=kv.at[dst], send_sem=kv_send.at[index], recv_sem=kv_recv.at[dst],
            device_id=device, device_id_type=MESH,
        )

    def kv_wait(slot):
        pltpu.make_async_remote_copy(
            src_ref=kv.at[slot], dst_ref=kv.at[slot], send_sem=kv_send.at[0], recv_sem=kv_recv.at[slot],
            device_id=pair, device_id_type=MESH,
        ).wait_recv()

    in_copies[0].wait()
    in_copies[1].wait()
    sends = []

    def kv_start(cond, src, dst, device):
        copy = kv_copy(src, dst, len(sends), device)
        sends.append((cond, copy))

        @pl.when(cond)
        def _():
            copy.start()

    kv_start(z < 3, 8, 4, at(z + 1, y))
    kv_start(z < 2, 8, 0, at(z + 2, y))
    for step in (1, 3, 2):
        yy = (y + step) % 4
        kv_start(yy > y, 8, 8 - jnp.maximum(yy - y, 0), at(z, yy))

    @pl.when(z >= 1)
    def _():
        kv_wait(4)

    for step in (1, 3, 2):
        yy = (y + step) % 4
        kv_start(z >= 1, 4, 4 - (yy - y), at(z, yy))

    @pl.when(z >= 2)
    def _():
        kv_wait(0)

    for step in (1, 3, 2):
        yy = (y + step) % 4
        kv_start((z >= 2) & (yy < y), 0, jnp.maximum(y - yy, 0), at(z, yy))

    for half in range(2):
        q_pos = s * TOK + half * HALF + lax.broadcasted_iota(jnp.int32, (HALF, 1), 0)
        start = jnp.zeros((HALF, 1), jnp.int32)
        edge = jnp.int32(0)
        for j in range(DOCS):
            start = jnp.where(q_pos >= edge, edge, start)
            edge = edge + len_ref[0, j]
        k_pos = (s - 8) * TOK + lax.broadcasted_iota(jnp.int32, (HALF, WINDOW * TOK), 1)
        seen = (k_pos <= q_pos) & (k_pos >= start)
        bias[pl.ds(half * HALF, HALF), :] = jnp.where(seen, 0.0, NEG).astype(F32)

    for slot in (1, 2, 3, 5, 6, 7):

        @pl.when(s - 8 + slot >= 0)
        def _():
            kv_wait(slot)

    for slot in range(WINDOW - 1):

        @pl.when(s - 8 + slot < 0)
        def _():
            kv[slot] = jnp.zeros((TOK, 512), BF16)

    in_copies[2].wait()

    factor = math.log2(math.e) / math.sqrt(HEAD)

    def attend(half):
        rows = pl.ds(half * HALF, HALF)
        for j in range(2):
            key = kv[:, :, j * HEAD : (j + 1) * HEAD].reshape(WINDOW * TOK, HEAD)
            value = kv[:, :, 256 + j * HEAD : 256 + (j + 1) * HEAD].reshape(WINDOW * TOK, HEAD)
            heads = [j * 8 + h for h in range(8)]
            query = jnp.concatenate([q_ref[rows, h * HEAD : (h + 1) * HEAD] for h in heads], axis=0)
            scores = lax.dot_general(query, key, (((1,), (1,)), ((), ())), preferred_element_type=F32)
            scores = (scores.reshape(8, HALF, WINDOW * TOK) + bias[rows, :][None]).reshape(8 * HALF, WINDOW * TOK)
            top = jnp.max(scores, axis=1, keepdims=True)
            expo = jnp.exp2((scores - top) * factor)
            total = jnp.sum(expo, axis=1, keepdims=True)
            blended = jnp.dot(expo.astype(BF16), value, preferred_element_type=F32) / total
            for i, h in enumerate(heads):
                gathered[s, rows, h * HEAD : (h + 1) * HEAD] = blended[i * HALF : (i + 1) * HALF].astype(BF16)

    def block(half, first, second):
        if half == 0:
            return ((z + first) % 4) * 4 + (y + second) % 4
        return ((z + second) % 4) * 4 + (y + first) % 4

    OFFSETS = (0, 0, 1, 3, 2)

    def ring_block(half, ring, offset):
        if ring == 0:
            return block(half, offset, 0)
        return block(half, OFFSETS[ring], offset)

    def neighbour(half, ring, offset):
        along_z = (half == 0) == (ring == 0)
        return at(z + offset, y) if along_z else at(z, y + offset)

    MOVES = ((0, 0, 1), (1, 0, 3), (1, 0, 1), (0, 0, 3), (0, 3, 1), (1, 1, 3))

    def ring_ref(half, ring, offset, piece):
        return gathered.at[ring_block(half, ring, offset), pl.ds(half * HALF + piece * PIECE, PIECE)]

    def ring_copy(half, ring, i):
        piece, origin, way = MOVES[i]
        ref = ring_ref(half, ring, origin, piece)
        return pltpu.make_async_remote_copy(
            src_ref=ref, dst_ref=ref, send_sem=g_send.at[half, ring, i], recv_sem=g_recv.at[half, ring, i],
            device_id=neighbour(half, ring, way), device_id_type=MESH,
        )

    def ring_start(half, ring, moves=(0, 1, 2, 3)):
        for i in moves:
            ring_copy(half, ring, i).start()

    def ring_wait(half, ring, moves):
        for i in moves:
            piece, origin, way = MOVES[i]
            ref = ring_ref(half, ring, (origin - way) % 4, piece)
            pltpu.make_async_remote_copy(
                src_ref=ref, dst_ref=ref, send_sem=g_send.at[half, ring, i], recv_sem=g_recv.at[half, ring, i],
                device_id=pair, device_id_type=MESH,
            ).wait_recv()

    def ring_forward(half, ring):
        for i in (0, 1):
            ring_wait(half, ring, (i,))
            ring_copy(half, ring, i + 4).start()

    def pair_copy(half, b):
        ref = (b % 8, pl.ds(half * HALF, HALF))
        return pltpu.make_async_remote_copy(
            src_ref=to_pair.at[ref], dst_ref=from_pair.at[ref],
            send_sem=p_send.at[half, b % 8], recv_sem=p_recv.at[half, b % 8],
            device_id=pair, device_id_type=MESH,
        )

    def far_copy(half, c):
        rows = pl.ds(half * HALF, HALF)
        return pltpu.make_async_remote_copy(
            src_ref=far.at[c, rows], dst_ref=result.at[2 * c + 1, rows],
            send_sem=x_send.at[half, c], recv_sem=x_recv.at[half, c],
            device_id=across, device_id_type=MESH,
        )

    waiting = []

    def combine(half, b):
        @pl.when(b // 8 == t)
        def _():
            c = b % 8
            rows = pl.ds(half * HALF, HALF)
            pair_copy(half, b).wait_recv()
            total = mine[c, rows] + from_pair[c, rows].astype(F32)
            pos = b * TOK + half * HALF + lax.broadcasted_iota(jnp.int32, (HALF, 1), 0)
            goal = jnp.zeros((HALF, 1), jnp.int32)
            edge = jnp.int32(0)
            for j in range(DOCS):
                goal = jnp.where(pos >= edge, dest_ref[0, j], goal)
                edge = edge + len_ref[0, j]
            result[2 * c, rows] = jnp.where(goal == x, total, 0.0).astype(BF16)
            far[c, rows] = jnp.where(goal == x, 0.0, total).astype(BF16)
            far_copy(half, c).start()

    def project(half, ring, offsets):
        blocks = [ring_block(half, ring, o) for o in offsets]
        rows = pl.ds(half * HALF, HALF)
        left = jnp.concatenate([gathered[b, rows] for b in blocks], axis=0)
        partial = jnp.dot(left, w_ref[...], preferred_element_type=F32)
        for i, b in enumerate(blocks):
            part = partial[i * HALF : (i + 1) * HALF]

            @pl.when(b // 8 == t)
            def _():
                mine[b % 8, rows] = part

            @pl.when(b // 8 != t)
            def _():
                to_pair[b % 8, rows] = part.astype(BF16)
                pair_copy(half, b).start()

        while waiting:
            combine(*waiting.pop())
        for b in blocks:
            waiting.append((half, b))

    for half in range(2):
        attend(half)
        ring_start(half, 0)
        ring_start(half, 1)
    for half in range(2):
        ring_forward(half, 0)
        ring_forward(half, 1)
    in_copies[3].wait()
    for half in range(2):
        ring_wait(half, 0, (2, 3))
        ring_start(half, 2)
        ring_start(half, 3)
        ring_wait(half, 1, (2, 3))
        project(half, 1, (1, 3))
    for half in range(2):
        ring_wait(half, 0, (4, 5))
        ring_start(half, 4)
        ring_wait(half, 1, (4, 5))
        project(half, 1, (0, 2))
    for ring in (2, 3, 4):
        for half in range(2):
            ring_forward(half, ring)
            ring_wait(half, ring, (2, 3))
            project(half, ring, (1, 3))
        for half in range(2):
            ring_wait(half, ring, (4, 5))
            project(half, ring, (0, 2))
    while waiting:
        combine(*waiting.pop())

    for half in range(2):
        for c in range(8):
            far_copy(half, c).wait_recv()
    out = pltpu.make_async_copy(result, out_hbm, out_sem)
    out.start()
    for cond, copy in sends:

        @pl.when(cond)
        def _():
            copy.wait_send()

    for half in range(2):
        for ring in range(5):
            for i in range(6):
                ring_copy(half, ring, i).wait_send()
        for c in range(8):
            far_copy(half, c).wait_send()
            pair_copy(half, c).wait_send()
    out.wait()


def shards(queries, keys, values, out_weight, doc_len, destination):
    dma = pltpu.SemaphoreType.DMA
    hbm = pl.BlockSpec(memory_space=pl.ANY)
    smem = pl.BlockSpec(memory_space=pltpu.SMEM)
    width = out_weight.shape[1]
    out = pl.pallas_call(
        kernel,
        out_shape=jax.ShapeDtypeStruct((16, TOK, width), BF16),
        in_specs=[hbm, hbm, hbm, hbm, smem, smem],
        out_specs=hbm,
        scratch_shapes=[
            pltpu.VMEM(queries.shape, BF16),
            pltpu.VMEM(out_weight.shape, BF16),
            pltpu.VMEM((WINDOW, TOK, 512), BF16),
            pltpu.VMEM((16, TOK, queries.shape[1]), BF16),
            pltpu.VMEM((TOK, WINDOW * TOK), F32),
            pltpu.VMEM((8, TOK, width), F32),
            pltpu.VMEM((8, TOK, width), BF16),
            pltpu.VMEM((8, TOK, width), BF16),
            pltpu.VMEM((8, TOK, width), BF16),
            pltpu.VMEM((16, TOK, width), BF16),
            dma((4,)),
            dma((11,)),
            dma((WINDOW,)),
            dma((2, 5, 6)),
            dma((2, 5, 6)),
            dma((2, 8)),
            dma((2, 8)),
            dma((2, 8)),
            dma((2, 8)),
            dma(()),
        ],
        compiler_params=pltpu.CompilerParams(
            collective_id=0, has_side_effects=True, vmem_limit_bytes=56 * 2**20
        ),
        cost_estimate=pl.CostEstimate(flops=6 * 10**9, bytes_accessed=6 * 2**20, transcendentals=3 * 10**6),
    )(queries, keys, values, out_weight, doc_len, destination)
    return out.reshape(16 * TOK, width)


def solution(mesh):
    in_specs = (
        P(("dp", "seq"), "tensor"),
        P(("dp", "seq"), "tensor"),
        P(("dp", "seq"), "tensor"),
        P("tensor", "seq"),
        P("dp", None),
        P("dp", None),
    )
    out_specs = P(("dp", "tensor"), "seq")
    return jax.shard_map(shards, mesh=mesh, in_specs=in_specs, out_specs=out_specs, check_vma=False)
```

time: 343 us -> 91.8 us (0.27)
  waiting for transfers between devices: 195 us -> 0 us
  Pallas kernels: 0 us -> 88.7 us
  matrix products: 66.7 us -> 0 us
  blocking collectives: 20.9 us -> 0 us
  other arithmetic: 17.9 us -> 0 us
  starting transfers between devices: 14.2 us -> 0 us
  between operations: 13.2 us -> 0.01 us
  local copies, waits for them, and re-layouts: 9.7 us -> 3.05 us
  loops' own time: 4.78 us -> 0 us
    all_gather x3 -> x0, waiting for transfers between devices: 169 us -> none  [the longest x1 121 us: shards(): lax.all_gather(heads_out, 'seq', axis=1, tiled=True)]
    pallas_call x0 -> x1, Pallas kernels: none -> 88.7 us  [shards(): pl.pallas_call(kernel, out_shape=jax.ShapeDtypeStruct((16, TOK, width), B...]
    dot_general x17 -> x0, matrix products: 66.7 us -> none  [the longest x8 29.8 us: block_scores(): jnp.einsum('qd,kd->qk', query_block, key_block, preferred_element_type=jn...]
    all_gather x1 -> x0, blocking collectives: 20.9 us -> none  [shards(): lax.all_gather(slot_info, 'seq', axis=1, tiled=True)]
    reduce_scatter x1 -> x0, waiting for transfers between devices: 15.4 us -> none  [reduce_groups(): lax.psum_scatter(total.astype(jnp.bfloat16), 'tensor', scatter_dimension=...]
    reduce_sum x10 -> x0, other arithmetic: 11.1 us -> none  [the longest x8 10.2 us: one_block(): total = jnp.sum(expo, axis=1, keepdims=True)]
    ppermute x4 -> x0, waiting for transfers between devices: 10.3 us -> none  [from_partner(): return lax.ppermute(block, axis, route)]
    ppermute x4 -> x0, starting transfers between devices: 9.77 us -> none  [from_partner(): return lax.ppermute(block, axis, route)]
  transfers between devices with their start and end apart: 9 -> 0, of which waited for: 7 -> 0; matrix products, arithmetic and copies ran while one was open for 3% -> 0% of each run, Pallas kernels for 0% -> 0%
where the time goes in v1:
time: 91.8 us; the launch traced here: 91.7 us
  Pallas kernels  88.7 us (97%)
  local copies, waits for them, and re-layouts  3.05 us (3%)
    pallas_call x1, Pallas kernels, shards(): pl.pallas_call(kernel, out_shape=jax.ShapeDtypeStruct((16, TOK, width), B...  88.7 us
    unnamed x1, local copies, waits for them, and re-layouts  3.05 us

profile of v1, /device:TPU:1, one launch (start us, length us, event | category | flops | bytes accessed | tf_op | source)
XLA Modules:
  0.0 91.7 jit_solution(18205646688635182394)
XLA Ops:
  0.0 88.7 %shard_map.64 = bf16[16,128,512]{2,1,0:T(8,128)(2,1)} custom-call(bf16[128,2048]{1,0:T(8,128)(2,1)} %q_hbm.1, bf16[128,256]{1,0:T(8,128)(2,1)} %k_hbm.1, bf16[128,256]{1,0:T(8,128)(2,1)} %v_hbm.1, bf16[2048,512]{1,0:T(8,128)(2,1)} %w_hbm.1, s32[1,16]{1,0:T(1,128)} %len_ref.1, s32[1,16]{1,0:T(1,128)} %dest_ref.1), custom_call_target="tpu_custom_call" | custom-call | flops 6000000000 | bytes 6291456 | tf_op jit(solution)/shard_map/pallas_call | solution.py:303
  88.7 3.0 %copy.8 = bf16[2048,512]{1,0:T(8,128)(2,1)} copy(bf16[2048,512]{1,0:T(8,128)(2,1)} %bitcast.1) | data formatting | bytes 4194304

commit v2 on v1

v2 whole, which is shorter than its diff:
```python
import math

import jax
import jax.numpy as jnp
from jax import lax
from jax.experimental import pallas as pl
from jax.experimental.pallas import tpu as pltpu
from jax.sharding import PartitionSpec as P

MESH = pl.DeviceIdType.MESH
HEAD = 128
TOK = 128
DOCS = 16
WINDOW = 9
HALF = TOK // 2
PIECE = TOK // 4
BF16 = jnp.bfloat16
F32 = jnp.float32
NEG = -1e30


def kernel(
    q_hbm, k_hbm, v_hbm, w_hbm, len_ref, dest_ref, result,
    q_ref, w_ref, kv, gathered, bias, mine, to_pair, from_pair, near, far,
    in_sems, kv_send, kv_recv, wz_send, wz_recv, wx_send, wx_recv, z_send, z_recv, y_send, y_recv,
    p_send, p_recv, n_send, n_recv, f_send, f_recv,
):
    x = lax.axis_index("dp")
    s = lax.axis_index("seq")
    t = lax.axis_index("tensor")
    z = s // 4
    y = s % 4
    side = z // 2
    inner = z % 2
    stays = t == side
    keep = jnp.where(stays, 0, 1)
    s_other = (s + 8) % 16
    s_to = jnp.where(stays, s, s_other)
    t_to = jnp.where(stays, t, 1 - t)

    def at(zz, yy):
        return (x, (zz % 4) * 4 + yy % 4, t)

    pair = (x, s, 1 - t)
    near_to = (x, s_to, t_to)
    far_to = ((x + 2) % 4, s_to, t_to)

    in_copies = [
        pltpu.make_async_copy(k_hbm, kv.at[WINDOW - 1, :, pl.ds(0, 256)], in_sems.at[0]),
        pltpu.make_async_copy(v_hbm, kv.at[WINDOW - 1, :, pl.ds(256, 256)], in_sems.at[1]),
        pltpu.make_async_copy(q_hbm, q_ref, in_sems.at[2]),
        pltpu.make_async_copy(w_hbm, w_ref.at[0], in_sems.at[3]),
    ]
    for copy in in_copies:
        copy.start()

    barrier = pltpu.get_barrier_semaphore()
    others = [at(z, y + 1), at(z, y + 2), at(z, y + 3), at(z + 1, y), at(z + 2, y), at(z + 3, y), pair]
    others += [((x + 1) % 4, s, t), ((x + 2) % 4, s, t), ((x + 3) % 4, s, t)]
    others += [(x, s_other, 1 - t), ((x + 2) % 4, s_other, 1 - t)]
    for other in others:
        pl.semaphore_signal(barrier, inc=1, device_id=other, device_id_type=MESH)
    pl.semaphore_wait(barrier, len(others))

    def kv_copy(src, dst, index, device):
        return pltpu.make_async_remote_copy(
            src_ref=kv.at[src], dst_ref=kv.at[dst], send_sem=kv_send.at[index], recv_sem=kv_recv.at[dst],
            device_id=device, device_id_type=MESH,
        )

    def kv_wait(slot):
        pltpu.make_async_remote_copy(
            src_ref=kv.at[slot], dst_ref=kv.at[slot], send_sem=kv_send.at[0], recv_sem=kv_recv.at[slot],
            device_id=pair, device_id_type=MESH,
        ).wait_recv()

    in_copies[0].wait()
    in_copies[1].wait()
    sends = []

    def kv_start(cond, src, dst, device):
        copy = kv_copy(src, dst, len(sends), device)
        sends.append((cond, copy))

        @pl.when(cond)
        def _():
            copy.start()

    kv_start(z < 3, 8, 4, at(z + 1, y))
    kv_start(z < 2, 8, 0, at(z + 2, y))
    for step in (1, 3, 2):
        yy = (y + step) % 4
        kv_start(yy > y, 8, 8 - jnp.maximum(yy - y, 0), at(z, yy))

    def w_rows(offset, part):
        return pl.ds((x + offset) % 4 * 512 + part * 128, 128)

    def wz_copy(part):
        return pltpu.make_async_remote_copy(
            src_ref=w_hbm.at[w_rows(0, part)], dst_ref=w_ref.at[1, w_rows(0, part)],
            send_sem=wz_send.at[part], recv_sem=wz_recv.at[part],
            device_id=at(z + 2, y), device_id_type=MESH,
        )

    def wx_copy(kind, part):
        origin = 0 if kind < 2 else (3 if part % 2 == 0 else 1)
        way = (1, 3, 1 if part % 2 == 0 else 3)[kind]
        ref = w_ref.at[1, w_rows(origin, part)]
        return pltpu.make_async_remote_copy(
            src_ref=ref, dst_ref=ref, send_sem=wx_send.at[kind, part], recv_sem=wx_recv.at[kind, part],
            device_id=((x + way) % 4, s, t), device_id_type=MESH,
        )

    def wx_wait(kind, part):
        offset = (3, 1, 2)[kind]
        ref = w_ref.at[1, w_rows(offset, part)]
        pltpu.make_async_remote_copy(
            src_ref=ref, dst_ref=ref, send_sem=wx_send.at[kind, part], recv_sem=wx_recv.at[kind, part],
            device_id=pair, device_id_type=MESH,
        ).wait_recv()

    def w_spread(part):
        wz_copy(part).wait_recv()
        wx_copy(0, part).start()
        wx_copy(1, part).start()

    def w_pass(part):
        wx_wait(part % 2, part)
        wx_copy(2, part).start()

    for part in range(4):
        wz_copy(part).start()

    @pl.when(z >= 1)
    def _():
        kv_wait(4)

    for step in (1, 3, 2):
        yy = (y + step) % 4
        kv_start(z >= 1, 4, 4 - (yy - y), at(z, yy))

    @pl.when(z >= 2)
    def _():
        kv_wait(0)

    for step in (1, 3, 2):
        yy = (y + step) % 4
        kv_start((z >= 2) & (yy < y), 0, jnp.maximum(y - yy, 0), at(z, yy))

    w_spread(0)
    w_spread(1)

    for half in range(2):
        q_pos = s * TOK + half * HALF + lax.broadcasted_iota(jnp.int32, (HALF, 1), 0)
        start = jnp.zeros((HALF, 1), jnp.int32)
        edge = jnp.int32(0)
        for j in range(DOCS):
            start = jnp.where(q_pos >= edge, edge, start)
            edge = edge + len_ref[0, j]
        k_pos = (s - 8) * TOK + lax.broadcasted_iota(jnp.int32, (HALF, WINDOW * TOK), 1)
        seen = (k_pos <= q_pos) & (k_pos >= start)
        bias[pl.ds(half * HALF, HALF), :] = jnp.where(seen, 0.0, NEG).astype(F32)

    for slot in (1, 2, 3, 5, 6, 7):

        @pl.when(s - 8 + slot >= 0)
        def _():
            kv_wait(slot)

    for slot in range(WINDOW - 1):

        @pl.when(s - 8 + slot < 0)
        def _():
            kv[slot] = jnp.zeros((TOK, 512), BF16)

    w_spread(2)
    in_copies[2].wait()

    own = inner * 4 + y
    factor = math.log2(math.e) / math.sqrt(HEAD)

    def attend(half):
        rows = pl.ds(half * HALF, HALF)
        for j in range(2):
            key = kv[:, :, j * HEAD : (j + 1) * HEAD].reshape(WINDOW * TOK, HEAD)
            value = kv[:, :, 256 + j * HEAD : 256 + (j + 1) * HEAD].reshape(WINDOW * TOK, HEAD)
            heads = [j * 8 + h for h in range(8)]
            query = jnp.concatenate([q_ref[rows, h * HEAD : (h + 1) * HEAD] for h in heads], axis=0)
            scores = lax.dot_general(query, key, (((1,), (1,)), ((), ())), preferred_element_type=F32)
            scores = (scores.reshape(8, HALF, WINDOW * TOK) + bias[rows, :][None]).reshape(8 * HALF, WINDOW * TOK)
            top = jnp.max(scores, axis=1, keepdims=True)
            expo = jnp.exp2((scores - top) * factor)
            total = jnp.sum(expo, axis=1, keepdims=True)
            blended = jnp.dot(expo.astype(BF16), value, preferred_element_type=F32) / total
            for i, h in enumerate(heads):
                gathered[own, rows, h * HEAD : (h + 1) * HEAD] = blended[i * HALF : (i + 1) * HALF].astype(BF16)

    def place(o, step):
        return (inner + o) % 2 * 4 + (y + step) % 4

    def piece_ref(o, step, piece):
        return gathered.at[place(o, step), pl.ds(piece * PIECE, PIECE)]

    def z_copy(piece):
        ref = piece_ref(0, 0, piece)
        return pltpu.make_async_remote_copy(
            src_ref=ref, dst_ref=ref, send_sem=z_send.at[piece], recv_sem=z_recv.at[piece],
            device_id=at(side * 2 + 1 - inner, y), device_id_type=MESH,
        )

    def y_copy(kind, o, piece):
        origin = 0 if kind < 2 else (3 if piece % 2 == 0 else 1)
        way = (1, 3, 1 if piece % 2 == 0 else 3)[kind]
        ref = piece_ref(o, origin, piece)
        return pltpu.make_async_remote_copy(
            src_ref=ref, dst_ref=ref, send_sem=y_send.at[kind, o, piece], recv_sem=y_recv.at[kind, o, piece],
            device_id=at(z, y + way), device_id_type=MESH,
        )

    arrived = set()

    def need(o, step, piece):
        if (o, step) == (0, 0) or (o, step, piece) in arrived:
            return
        arrived.add((o, step, piece))
        ref = piece_ref(o, step, piece)
        if step == 0:
            send, recv = z_send.at[piece], z_recv.at[piece]
        else:
            kind = {3: 0, 1: 1, 2: 2}[step]
            send, recv = y_send.at[kind, o, piece], y_recv.at[kind, o, piece]
        pltpu.make_async_remote_copy(
            src_ref=ref, dst_ref=ref, send_sem=send, recv_sem=recv, device_id=pair, device_id_type=MESH
        ).wait_recv()

    def y_start(o, *pieces):
        for a, b in pieces:
            need(o, 0, a)
            need(o, 0, b)
            y_copy(0, o, a).start()
            y_copy(1, o, b).start()

    def y_pass(o, *pieces):
        for piece in pieces:
            need(o, 3 if piece % 2 == 0 else 1, piece)
            y_copy(2, o, piece).start()

    def pair_copy(half, c):
        ref = (c, pl.ds(half * HALF, HALF))
        return pltpu.make_async_remote_copy(
            src_ref=to_pair.at[ref], dst_ref=from_pair.at[ref],
            send_sem=p_send.at[half, c], recv_sem=p_recv.at[half, c],
            device_id=pair, device_id_type=MESH,
        )

    def near_copy(half, c):
        rows = pl.ds(half * HALF, HALF)
        return pltpu.make_async_remote_copy(
            src_ref=near.at[c, rows], dst_ref=result.at[2 * c, rows],
            send_sem=n_send.at[half, c], recv_sem=n_recv.at[half, c],
            device_id=near_to, device_id_type=MESH,
        )

    def far_copy(half, c):
        rows = pl.ds(half * HALF, HALF)
        return pltpu.make_async_remote_copy(
            src_ref=far.at[c, rows], dst_ref=result.at[2 * c + 1, rows],
            send_sem=f_send.at[half, c], recv_sem=f_recv.at[half, c],
            device_id=far_to, device_id_type=MESH,
        )

    waiting = []

    def combine(half, c):
        rows = pl.ds(half * HALF, HALF)
        pair_copy(half, c).wait_recv()
        total = mine[c, rows] + from_pair[c, rows].astype(F32)
        pos = (side * 8 + c) * TOK + half * HALF + lax.broadcasted_iota(jnp.int32, (HALF, 1), 0)
        goal = jnp.zeros((HALF, 1), jnp.int32)
        edge = jnp.int32(0)
        for j in range(DOCS):
            goal = jnp.where(pos >= edge, dest_ref[0, j], goal)
            edge = edge + len_ref[0, j]
        far[c, rows] = jnp.where(goal == x, 0.0, total).astype(BF16)
        far_copy(half, c).start()
        kept = jnp.where(goal == x, total, 0.0).astype(BF16)

        @pl.when(stays)
        def _():
            result[2 * c, rows] = kept

        @pl.when(jnp.logical_not(stays))
        def _():
            near[c, rows] = kept
            near_copy(half, c).start()

    def project(*parts):
        for o, step, half in parts:
            for piece in (2 * half, 2 * half + 1):
                need(o, step, piece)
        places = [(place(o, step), pl.ds(half * HALF, HALF)) for o, step, half in parts]
        left = [gathered[c, rows] for c, rows in places]
        left = left[0] if len(left) == 1 else jnp.concatenate(left, axis=0)
        given = jnp.dot(left, w_ref[1 - keep], preferred_element_type=F32)
        for i, ((c, rows), (_, _, half)) in enumerate(zip(places, parts)):
            to_pair[c, rows] = given[i * HALF : (i + 1) * HALF].astype(BF16)
            pair_copy(half, c).start()
        kept = jnp.dot(left, w_ref[keep], preferred_element_type=F32)
        for i, (c, rows) in enumerate(places):
            mine[c, rows] = kept[i * HALF : (i + 1) * HALF]
        while waiting:
            combine(*waiting.pop(0))
        for (c, _), (_, _, half) in zip(places, parts):
            waiting.append((half, c))

    attend(0)
    z_copy(0).start()
    z_copy(1).start()
    y_start(0, (0, 1), (1, 0))
    w_spread(3)
    w_pass(0)
    attend(1)
    z_copy(2).start()
    z_copy(3).start()
    y_start(0, (2, 3), (3, 2))
    w_pass(1)
    w_pass(2)
    y_start(1, (0, 1))
    y_pass(0, 0, 1)
    y_start(1, (1, 0))
    w_pass(3)
    y_start(1, (2, 3))
    in_copies[3].wait()
    for part in range(4):
        wx_wait(1 - part % 2, part)
        wx_wait(2, part)
    project((0, 0, 0), (0, 0, 1))
    y_pass(1, 0, 1)
    y_start(1, (3, 2))
    project((0, 1, 0), (0, 3, 0))
    y_pass(0, 2, 3)
    project((1, 0, 0), (1, 0, 1))
    y_pass(1, 2, 3)
    project((0, 1, 1), (0, 3, 1))
    project((1, 1, 0), (1, 3, 0))
    project((0, 2, 0), (1, 2, 0))
    project((1, 1, 1), (1, 3, 1))
    project((0, 2, 1))
    project((1, 2, 1))
    while waiting:
        combine(*waiting.pop(0))

    for half in range(2):
        for c in range(8):
            far_copy(half, c).wait()
            pair_copy(half, c).wait_send()

            @pl.when(jnp.logical_not(stays))
            def _():
                near_copy(half, c).wait()

    for cond, copy in sends:

        @pl.when(cond)
        def _():
            copy.wait_send()

    for part in range(4):
        wz_copy(part).wait_send()
        z_copy(part).wait_send()
        for kind in range(3):
            wx_copy(kind, part).wait_send()
            for o in range(2):
                y_copy(kind, o, part).wait_send()


def shards(queries, keys, values, out_weight, doc_len, destination):
    dma = pltpu.SemaphoreType.DMA
    hbm = pl.BlockSpec(memory_space=pl.ANY)
    smem = pl.BlockSpec(memory_space=pltpu.SMEM)
    width = out_weight.shape[1]
    out = pl.pallas_call(
        kernel,
        out_shape=pltpu.VMEM((16, TOK, width), BF16),
        in_specs=[hbm, hbm, hbm, hbm, smem, smem],
        out_specs=pl.BlockSpec(memory_space=pltpu.VMEM),
        scratch_shapes=[
            pltpu.VMEM(queries.shape, BF16),
            pltpu.VMEM((2,) + out_weight.shape, BF16),
            pltpu.VMEM((WINDOW, TOK, 512), BF16),
            pltpu.VMEM((8, TOK, queries.shape[1]), BF16),
            pltpu.VMEM((TOK, WINDOW * TOK), F32),
            pltpu.VMEM((8, TOK, width), F32),
            pltpu.VMEM((8, TOK, width), BF16),
            pltpu.VMEM((8, TOK, width), BF16),
            pltpu.VMEM((8, TOK, width), BF16),
            pltpu.VMEM((8, TOK, width), BF16),
            dma((4,)),
            dma((11,)),
            dma((WINDOW,)),
            dma((4,)),
            dma((4,)),
            dma((3, 4)),
            dma((3, 4)),
            dma((4,)),
            dma((4,)),
            dma((3, 2, 4)),
            dma((3, 2, 4)),
            dma((2, 8)),
            dma((2, 8)),
            dma((2, 8)),
            dma((2, 8)),
            dma((2, 8)),
            dma((2, 8)),
        ],
        compiler_params=pltpu.CompilerParams(
            collective_id=0, has_side_effects=True, vmem_limit_bytes=56 * 2**20
        ),
        cost_estimate=pl.CostEstimate(flops=6 * 10**9, bytes_accessed=6 * 2**20, transcendentals=3 * 10**6),
    )(queries, keys, values, out_weight, doc_len, destination)
    return out.reshape(16 * TOK, width)


def solution(mesh):
    in_specs = (
        P(("dp", "seq"), "tensor"),
        P(("dp", "seq"), "tensor"),
        P(("dp", "seq"), "tensor"),
        P("tensor", "seq"),
        P("dp", None),
        P("dp", None),
    )
    out_specs = P(("dp", "tensor"), "seq")
    return jax.shard_map(shards, mesh=mesh, in_specs=in_specs, out_specs=out_specs, check_vma=False)
```

time: 91.8 us -> 79.8 us (0.87)
  Pallas kernels: 88.7 us -> 78.3 us
  local copies, waits for them, and re-layouts: 3.05 us -> 1.32 us
    pallas_call x1, Pallas kernels: 88.7 us -> 78.3 us  [shards(): pl.pallas_call(kernel, out_shape=pltpu.VMEM((16, TOK, width), BF16), in_s...]
    unnamed x1, local copies, waits for them, and re-layouts: 3.05 us -> 1.32 us
where the time goes in v2:
time: 79.8 us; the launch traced here: 79.7 us
  Pallas kernels  78.3 us (98%)
  local copies, waits for them, and re-layouts  1.32 us (2%)
    pallas_call x1, Pallas kernels, shards(): pl.pallas_call(kernel, out_shape=pltpu.VMEM((16, TOK, width), BF16), in_s...  78.3 us

profile of v2, /device:TPU:1, one launch (start us, length us, event | category | flops | bytes accessed | tf_op | source)
XLA Modules:
  0.0 79.7 jit_solution(9916531562514854902)
XLA Ops:
  0.0 78.3 %shard_map.64 = bf16[16,128,512]{2,1,0:T(8,128)(2,1)S(1)} custom-call(bf16[128,2048]{1,0:T(8,128)(2,1)} %q_hbm.1, bf16[128,256]{1,0:T(8,128)(2,1)} %k_hbm.1, bf16[128,256]{1,0:T(8,128)(2,1)} %v_hbm.1, bf16[2048,512]{1,0:T(8,128)(2,1)} %w_hbm.1, s32[1,16]{1,0:T(1,128)} %len_ref.1, s32[1,16]{1,0:T(1,128)} %dest_ref.1), custom_call_target="tpu_custom_call" | custom-call | flops 6000000000 | bytes 6291456 | tf_op jit(solution)/shard_map/pallas_call | solution.py:382
  78.4 1.3 %copy.8 = bf16[2048,512]{1,0:T(8,128)(2,1)} copy(bf16[2048,512]{1,0:T(8,128)(2,1)S(1)} %bitcast.1) | data formatting | bytes 4194304

commit v3 on v2

--- a/solution.py
+++ b/solution.py
@@ -13,7 +13,6 @@
 DOCS = 16
 WINDOW = 9
 HALF = TOK // 2
-PIECE = TOK // 4
 BF16 = jnp.bfloat16
 F32 = jnp.float32
 NEG = -1e30
@@ -46,10 +45,15 @@
     far_to = ((x + 2) % 4, s_to, t_to)
 
     in_copies = [
-        pltpu.make_async_copy(k_hbm, kv.at[WINDOW - 1, :, pl.ds(0, 256)], in_sems.at[0]),
-        pltpu.make_async_copy(v_hbm, kv.at[WINDOW - 1, :, pl.ds(256, 256)], in_sems.at[1]),
-        pltpu.make_async_copy(q_hbm, q_ref, in_sems.at[2]),
-        pltpu.make_async_copy(w_hbm, w_ref.at[0], in_sems.at[3]),
+        pltpu.make_async_copy(
+            ref.at[:, pl.ds(j * HEAD, HEAD)], kv.at[WINDOW - 1, j, :, pl.ds(n * HEAD, HEAD)], in_sems.at[2 * j + n]
+        )
+        for j in range(2)
+        for n, ref in enumerate((k_hbm, v_hbm))
+    ]
+    in_copies += [
+        pltpu.make_async_copy(q_hbm, q_ref, in_sems.at[4]),
+        pltpu.make_async_copy(w_hbm, w_ref.at[0], in_sems.at[5]),
     ]
     for copy in in_copies:
         copy.start()
@@ -62,35 +66,60 @@
         pl.semaphore_signal(barrier, inc=1, device_id=other, device_id_type=MESH)
     pl.semaphore_wait(barrier, len(others))
 
-    def kv_copy(src, dst, index, device):
-        return pltpu.make_async_remote_copy(
-            src_ref=kv.at[src], dst_ref=kv.at[dst], send_sem=kv_send.at[index], recv_sem=kv_recv.at[dst],
+    def kv_copy(head, src, dst, index, device):
+        return pltpu.make_async_remote_copy(
+            src_ref=kv.at[src, head], dst_ref=kv.at[dst, head],
+            send_sem=kv_send.at[head, index], recv_sem=kv_recv.at[head, dst],
             device_id=device, device_id_type=MESH,
         )
 
-    def kv_wait(slot):
-        pltpu.make_async_remote_copy(
-            src_ref=kv.at[slot], dst_ref=kv.at[slot], send_sem=kv_send.at[0], recv_sem=kv_recv.at[slot],
-            device_id=pair, device_id_type=MESH,
-        ).wait_recv()
-
-    in_copies[0].wait()
-    in_copies[1].wait()
+    def kv_wait(head, slot):
+        @pl.when(s - 8 + slot >= 0)
+        def _():
+            pltpu.make_async_remote_copy(
+                src_ref=kv.at[slot, head], dst_ref=kv.at[slot, head],
+                send_sem=kv_send.at[head, 0], recv_sem=kv_recv.at[head, slot],
+                device_id=pair, device_id_type=MESH,
+            ).wait_recv()
+
     sends = []
 
-    def kv_start(cond, src, dst, device):
-        copy = kv_copy(src, dst, len(sends), device)
+    def kv_start(head, index, cond, src, dst, device):
+        copy = kv_copy(head, src, dst, index, device)
         sends.append((cond, copy))
 
         @pl.when(cond)
         def _():
             copy.start()
 
-    kv_start(z < 3, 8, 4, at(z + 1, y))
-    kv_start(z < 2, 8, 0, at(z + 2, y))
-    for step in (1, 3, 2):
-        yy = (y + step) % 4
-        kv_start(yy > y, 8, 8 - jnp.maximum(yy - y, 0), at(z, yy))
+    steps = [(n, (y + step) % 4) for n, step in enumerate((1, 3, 2))]
+
+    def kv_column(head):
+        in_copies[2 * head].wait()
+        in_copies[2 * head + 1].wait()
+        kv_start(head, 0, z < 3, 8, 4, at(z + 1, y))
+        kv_start(head, 1, z < 2, 8, 0, at(z + 2, y))
+
+    def kv_row(head):
+        for n, yy in steps:
+            kv_start(head, 2 + n, yy > y, 8, 8 - jnp.maximum(yy - y, 0), at(z, yy))
+
+    def kv_relay(head):
+        kv_wait(head, 4)
+        for n, yy in steps:
+            kv_start(head, 5 + n, z >= 1, 4, 4 - (yy - y), at(z, yy))
+        kv_wait(head, 0)
+        for n, yy in steps:
+            kv_start(head, 8 + n, (z >= 2) & (yy < y), 0, jnp.maximum(y - yy, 0), at(z, yy))
+
+    def kv_rest(head):
+        for slot in (5, 6, 7, 1, 2, 3):
+            kv_wait(head, slot)
+        for slot in range(WINDOW - 1):
+
+            @pl.when(s - 8 + slot < 0)
+            def _():
+                kv[slot, head] = jnp.zeros((TOK, 2 * HEAD), BF16)
 
     def w_rows(offset, part):
         return pl.ds((x + offset) % 4 * 512 + part * 128, 128)
@@ -128,27 +157,16 @@
         wx_wait(part % 2, part)
         wx_copy(2, part).start()
 
-    for part in range(4):
+
+    kv_column(0)
+    kv_row(0)
+    wz_copy(0).start()
+    kv_column(1)
+    for part in range(1, 4):
         wz_copy(part).start()
-
-    @pl.when(z >= 1)
-    def _():
-        kv_wait(4)
-
-    for step in (1, 3, 2):
-        yy = (y + step) % 4
-        kv_start(z >= 1, 4, 4 - (yy - y), at(z, yy))
-
-    @pl.when(z >= 2)
-    def _():
-        kv_wait(0)
-
-    for step in (1, 3, 2):
-        yy = (y + step) % 4
-        kv_start((z >= 2) & (yy < y), 0, jnp.maximum(y - yy, 0), at(z, yy))
-
-    w_spread(0)
-    w_spread(1)
+    kv_relay(0)
+    kv_row(1)
+    kv_relay(1)
 
     for half in range(2):
         q_pos = s * TOK + half * HALF + lax.broadcasted_iota(jnp.int32, (HALF, 1), 0)
@@ -161,45 +179,30 @@
         seen = (k_pos <= q_pos) & (k_pos >= start)
         bias[pl.ds(half * HALF, HALF), :] = jnp.where(seen, 0.0, NEG).astype(F32)
 
-    for slot in (1, 2, 3, 5, 6, 7):
-
-        @pl.when(s - 8 + slot >= 0)
-        def _():
-            kv_wait(slot)
-
-    for slot in range(WINDOW - 1):
-
-        @pl.when(s - 8 + slot < 0)
-        def _():
-            kv[slot] = jnp.zeros((TOK, 512), BF16)
-
-    w_spread(2)
-    in_copies[2].wait()
+    in_copies[4].wait()
 
     own = inner * 4 + y
     factor = math.log2(math.e) / math.sqrt(HEAD)
 
-    def attend(half):
+    def attend(half, j):
         rows = pl.ds(half * HALF, HALF)
-        for j in range(2):
-            key = kv[:, :, j * HEAD : (j + 1) * HEAD].reshape(WINDOW * TOK, HEAD)
-            value = kv[:, :, 256 + j * HEAD : 256 + (j + 1) * HEAD].reshape(WINDOW * TOK, HEAD)
-            heads = [j * 8 + h for h in range(8)]
-            query = jnp.concatenate([q_ref[rows, h * HEAD : (h + 1) * HEAD] for h in heads], axis=0)
-            scores = lax.dot_general(query, key, (((1,), (1,)), ((), ())), preferred_element_type=F32)
-            scores = (scores.reshape(8, HALF, WINDOW * TOK) + bias[rows, :][None]).reshape(8 * HALF, WINDOW * TOK)
-            top = jnp.max(scores, axis=1, keepdims=True)
-            expo = jnp.exp2((scores - top) * factor)
-            total = jnp.sum(expo, axis=1, keepdims=True)
-            blended = jnp.dot(expo.astype(BF16), value, preferred_element_type=F32) / total
-            for i, h in enumerate(heads):
-                gathered[own, rows, h * HEAD : (h + 1) * HEAD] = blended[i * HALF : (i + 1) * HALF].astype(BF16)
+        key = kv[:, j, :, :HEAD].reshape(WINDOW * TOK, HEAD)
+        value = kv[:, j, :, HEAD:].reshape(WINDOW * TOK, HEAD)
+        query = jnp.concatenate([q_ref[rows, (j * 8 + h) * HEAD : (j * 8 + h + 1) * HEAD] for h in range(8)], axis=0)
+        scores = lax.dot_general(query, key, (((1,), (1,)), ((), ())), preferred_element_type=F32)
+        scores = (scores.reshape(8, HALF, WINDOW * TOK) + bias[rows, :][None]).reshape(8 * HALF, WINDOW * TOK)
+        top = jnp.max(scores, axis=1, keepdims=True)
+        expo = jnp.exp2((scores - top) * factor)
+        total = jnp.sum(expo, axis=1, keepdims=True)
+        blended = jnp.dot(expo.astype(BF16), value, preferred_element_type=F32) / total
+        for h in range(8):
+            gathered[own, j, rows, h * HEAD : (h + 1) * HEAD] = blended[h * HALF : (h + 1) * HALF].astype(BF16)
 
     def place(o, step):
         return (inner + o) % 2 * 4 + (y + step) % 4
 
     def piece_ref(o, step, piece):
-        return gathered.at[place(o, step), pl.ds(piece * PIECE, PIECE)]
+        return gathered.at[place(o, step), piece % 2, pl.ds(piece // 2 * HALF, HALF)]
 
     def z_copy(piece):
         ref = piece_ref(0, 0, piece)
@@ -269,7 +272,7 @@
             device_id=far_to, device_id_type=MESH,
         )
 
-    waiting = []
+    done = []
 
     def combine(half, c):
         rows = pl.ds(half * HALF, HALF)
@@ -299,7 +302,7 @@
             for piece in (2 * half, 2 * half + 1):
                 need(o, step, piece)
         places = [(place(o, step), pl.ds(half * HALF, HALF)) for o, step, half in parts]
-        left = [gathered[c, rows] for c, rows in places]
+        left = [jnp.concatenate([gathered[c, 0, rows], gathered[c, 1, rows]], axis=1) for c, rows in places]
         left = left[0] if len(left) == 1 else jnp.concatenate(left, axis=0)
         given = jnp.dot(left, w_ref[1 - keep], preferred_element_type=F32)
         for i, ((c, rows), (_, _, half)) in enumerate(zip(places, parts)):
@@ -308,57 +311,57 @@
         kept = jnp.dot(left, w_ref[keep], preferred_element_type=F32)
         for i, (c, rows) in enumerate(places):
             mine[c, rows] = kept[i * HALF : (i + 1) * HALF]
-        while waiting:
-            combine(*waiting.pop(0))
         for (c, _), (_, _, half) in zip(places, parts):
-            waiting.append((half, c))
-
-    attend(0)
+            combine(half, c)
+            done.append((half, c))
+
+    def finish(half, c):
+        pair_copy(half, c).wait_send()
+        far_copy(half, c).wait()
+
+        @pl.when(jnp.logical_not(stays))
+        def _():
+            near_copy(half, c).wait()
+
+    w_spread(0)
+    kv_rest(0)
+    attend(0, 0)
     z_copy(0).start()
+    y_copy(0, 0, 0).start()
+    y_copy(1, 0, 0).start()
+    w_spread(1)
+    attend(1, 0)
+    z_copy(2).start()
+    kv_rest(1)
+    attend(0, 1)
     z_copy(1).start()
-    y_start(0, (0, 1), (1, 0))
+    y_copy(0, 0, 1).start()
+    y_copy(1, 0, 1).start()
+    w_spread(2)
+    w_pass(0)
+    attend(1, 1)
+    z_copy(3).start()
     w_spread(3)
-    w_pass(0)
-    attend(1)
-    z_copy(2).start()
-    z_copy(3).start()
+    w_pass(1)
+    y_start(1, (0, 1), (1, 0))
+    y_pass(0, 0, 1)
+    w_pass(2)
     y_start(0, (2, 3), (3, 2))
-    w_pass(1)
-    w_pass(2)
-    y_start(1, (0, 1))
-    y_pass(0, 0, 1)
-    y_start(1, (1, 0))
     w_pass(3)
-    y_start(1, (2, 3))
-    in_copies[3].wait()
+    y_pass(1, 0, 1)
+    in_copies[5].wait()
     for part in range(4):
         wx_wait(1 - part % 2, part)
         wx_wait(2, part)
     project((0, 0, 0), (0, 0, 1))
-    y_pass(1, 0, 1)
-    y_start(1, (3, 2))
     project((0, 1, 0), (0, 3, 0))
+    y_start(1, (2, 3), (3, 2))
+    project((1, 0, 0), (1, 0, 1))
     y_pass(0, 2, 3)
-    project((1, 0, 0), (1, 0, 1))
+    project((1, 1, 0), (1, 3, 0))
+    project((0, 2, 0), (1, 2, 0))
     y_pass(1, 2, 3)
     project((0, 1, 1), (0, 3, 1))
-    project((1, 1, 0), (1, 3, 0))
-    project((0, 2, 0), (1, 2, 0))
-    project((1, 1, 1), (1, 3, 1))
-    project((0, 2, 1))
-    project((1, 2, 1))
-    while waiting:
-        combine(*waiting.pop(0))
-
-    for half in range(2):
-        for c in range(8):
-            far_copy(half, c).wait()
-            pair_copy(half, c).wait_send()
-
-            @pl.when(jnp.logical_not(stays))
-            def _():
-                near_copy(half, c).wait()
-
     for cond, copy in sends:
 
         @pl.when(cond)
@@ -370,8 +373,17 @@
         z_copy(part).wait_send()
         for kind in range(3):
             wx_copy(kind, part).wait_send()
-            for o in range(2):
-                y_copy(kind, o, part).wait_send()
+            y_copy(kind, 0, part).wait_send()
+    project((1, 1, 1), (1, 3, 1))
+    for half, c in done[:8]:
+        finish(half, c)
+    project((0, 2, 1))
+    project((1, 2, 1))
+    for part in range(4):
+        for kind in range(3):
+            y_copy(kind, 1, part).wait_send()
+    for half, c in done[8:]:
+        finish(half, c)
 
 
 def shards(queries, keys, values, out_weight, doc_len, destination):
@@ -387,17 +399,17 @@
         scratch_shapes=[
             pltpu.VMEM(queries.shape, BF16),
             pltpu.VMEM((2,) + out_weight.shape, BF16),
-            pltpu.VMEM((WINDOW, TOK, 512), BF16),
-            pltpu.VMEM((8, TOK, queries.shape[1]), BF16),
+            pltpu.VMEM((WINDOW, 2, TOK, 2 * HEAD), BF16),
+            pltpu.VMEM((8, 2, TOK, queries.shape[1] // 2), BF16),
             pltpu.VMEM((TOK, WINDOW * TOK), F32),
             pltpu.VMEM((8, TOK, width), F32),
             pltpu.VMEM((8, TOK, width), BF16),
             pltpu.VMEM((8, TOK, width), BF16),
             pltpu.VMEM((8, TOK, width), BF16),
             pltpu.VMEM((8, TOK, width), BF16),
-            dma((4,)),
-            dma((11,)),
-            dma((WINDOW,)),
+            dma((6,)),
+            dma((2, 11)),
+            dma((2, WINDOW)),
             dma((4,)),
             dma((4,)),
             dma((3, 4)),

time: 79.8 us -> 73.6 us (0.922)
  Pallas kernels: 78.3 us -> 72 us
    pallas_call x1, Pallas kernels: 78.3 us -> 72 us  [shards(): pl.pallas_call(kernel, out_shape=pltpu.VMEM((16, TOK, width), BF16), in_s...]
where the time goes in v3:
time: 73.6 us; the launch traced here: 73.3 us
  Pallas kernels  72 us (98%)
  local copies, waits for them, and re-layouts  1.32 us (2%)
    pallas_call x1, Pallas kernels, shards(): pl.pallas_call(kernel, out_shape=pltpu.VMEM((16, TOK, width), BF16), in_s...  72 us

profile of v3, /device:TPU:1, one launch (start us, length us, event | category | flops | bytes accessed | tf_op | source)
XLA Modules:
  0.0 73.3 jit_solution(6712832725514502684)
XLA Ops:
  0.0 72.0 %shard_map.64 = bf16[16,128,512]{2,1,0:T(8,128)(2,1)S(1)} custom-call(bf16[128,2048]{1,0:T(8,128)(2,1)} %q_hbm.1, bf16[128,256]{1,0:T(8,128)(2,1)} %k_hbm.1, bf16[128,256]{1,0:T(8,128)(2,1)} %v_hbm.1, bf16[2048,512]{1,0:T(8,128)(2,1)} %w_hbm.1, s32[1,16]{1,0:T(1,128)} %len_ref.1, s32[1,16]{1,0:T(1,128)} %dest_ref.1), custom_call_target="tpu_custom_call" | custom-call | flops 6000000000 | bytes 6291456 | tf_op jit(solution)/shard_map/pallas_call | solution.py:394
  72.0 1.3 %copy.8 = bf16[2048,512]{1,0:T(8,128)(2,1)} copy(bf16[2048,512]{1,0:T(8,128)(2,1)S(1)} %bitcast.1) | data formatting | bytes 4194304

commit v4 on v3

--- a/solution.py
+++ b/solution.py
@@ -331,10 +331,10 @@
     y_copy(1, 0, 0).start()
     w_spread(1)
     attend(1, 0)
-    z_copy(2).start()
     kv_rest(1)
     attend(0, 1)
     z_copy(1).start()
+    z_copy(2).start()
     y_copy(0, 0, 1).start()
     y_copy(1, 0, 1).start()
     w_spread(2)
@@ -343,8 +343,10 @@
     z_copy(3).start()
     w_spread(3)
     w_pass(1)
-    y_start(1, (0, 1), (1, 0))
-    y_pass(0, 0, 1)
+    y_start(1, (0, 0))
+    y_pass(0, 0)
+    y_start(1, (1, 1))
+    y_pass(0, 1)
     w_pass(2)
     y_start(0, (2, 3), (3, 2))
     w_pass(3)

time: 73.6 us -> 73.4 us (level)
  no operation moved by 1% of the time
where the time goes in v4:
time: 73.4 us; the launch traced here: 73.3 us
  Pallas kernels  72 us (98%)
  local copies, waits for them, and re-layouts  1.32 us (2%)
    pallas_call x1, Pallas kernels, shards(): pl.pallas_call(kernel, out_shape=pltpu.VMEM((16, TOK, width), BF16), in_s...  72 us

profile of v4, /device:TPU:1, one launch (start us, length us, event | category | flops | bytes accessed | tf_op | source)
XLA Modules:
  0.0 73.3 jit_solution(9544919523542810303)
XLA Ops:
  0.0 72.0 %shard_map.64 = bf16[16,128,512]{2,1,0:T(8,128)(2,1)S(1)} custom-call(bf16[128,2048]{1,0:T(8,128)(2,1)} %q_hbm.1, bf16[128,256]{1,0:T(8,128)(2,1)} %k_hbm.1, bf16[128,256]{1,0:T(8,128)(2,1)} %v_hbm.1, bf16[2048,512]{1,0:T(8,128)(2,1)} %w_hbm.1, s32[1,16]{1,0:T(1,128)} %len_ref.1, s32[1,16]{1,0:T(1,128)} %dest_ref.1), custom_call_target="tpu_custom_call" | custom-call | flops 6000000000 | bytes 6291456 | tf_op jit(solution)/shard_map/pallas_call | solution.py:396
  72.0 1.3 %copy.8 = bf16[2048,512]{1,0:T(8,128)(2,1)} copy(bf16[2048,512]{1,0:T(8,128)(2,1)S(1)} %bitcast.1) | data formatting | bytes 4194304

commit v5 on v4

--- a/solution.py
+++ b/solution.py
@@ -276,17 +276,18 @@
 
     def combine(half, c):
         rows = pl.ds(half * HALF, HALF)
-        pair_copy(half, c).wait_recv()
-        total = mine[c, rows] + from_pair[c, rows].astype(F32)
         pos = (side * 8 + c) * TOK + half * HALF + lax.broadcasted_iota(jnp.int32, (HALF, 1), 0)
         goal = jnp.zeros((HALF, 1), jnp.int32)
         edge = jnp.int32(0)
         for j in range(DOCS):
             goal = jnp.where(pos >= edge, dest_ref[0, j], goal)
             edge = edge + len_ref[0, j]
-        far[c, rows] = jnp.where(goal == x, 0.0, total).astype(BF16)
+        here = jnp.broadcast_to(goal == x, (HALF, far.shape[2]))
+        pair_copy(half, c).wait_recv()
+        total = mine[c, rows] + from_pair[c, rows].astype(F32)
+        far[c, rows] = jnp.where(here, 0.0, total).astype(BF16)
         far_copy(half, c).start()
-        kept = jnp.where(goal == x, total, 0.0).astype(BF16)
+        kept = jnp.where(here, total, 0.0).astype(BF16)
 
         @pl.when(stays)
         def _():
@@ -362,8 +363,8 @@
     y_pass(0, 2, 3)
     project((1, 1, 0), (1, 3, 0))
     project((0, 2, 0), (1, 2, 0))
+    project((0, 1, 1), (0, 3, 1))
     y_pass(1, 2, 3)
-    project((0, 1, 1), (0, 3, 1))
     for cond, copy in sends:
 
         @pl.when(cond)
@@ -377,14 +378,12 @@
             wx_copy(kind, part).wait_send()
             y_copy(kind, 0, part).wait_send()
     project((1, 1, 1), (1, 3, 1))
-    for half, c in done[:8]:
-        finish(half, c)
     project((0, 2, 1))
     project((1, 2, 1))
     for part in range(4):
         for kind in range(3):
             y_copy(kind, 1, part).wait_send()
-    for half, c in done[8:]:
+    for half, c in done:
         finish(half, c)
 
 

time: 73.4 us -> 73.4 us (level)
  no operation moved by 1% of the time
where the time goes in v5:
time: 73.4 us; the launch traced here: 73.3 us
  Pallas kernels  72 us (98%)
  local copies, waits for them, and re-layouts  1.32 us (2%)
    pallas_call x1, Pallas kernels, shards(): pl.pallas_call(kernel, out_shape=pltpu.VMEM((16, TOK, width), BF16), in_s...  72 us

profile of v5, /device:TPU:1, one launch (start us, length us, event | category | flops | bytes accessed | tf_op | source)
XLA Modules:
  0.0 73.3 jit_solution(2862857220815399652)
XLA Ops:
  0.0 72.0 %shard_map.64 = bf16[16,128,512]{2,1,0:T(8,128)(2,1)S(1)} custom-call(bf16[128,2048]{1,0:T(8,128)(2,1)} %q_hbm.1, bf16[128,256]{1,0:T(8,128)(2,1)} %k_hbm.1, bf16[128,256]{1,0:T(8,128)(2,1)} %v_hbm.1, bf16[2048,512]{1,0:T(8,128)(2,1)} %w_hbm.1, s32[1,16]{1,0:T(1,128)} %len_ref.1, s32[1,16]{1,0:T(1,128)} %dest_ref.1), custom_call_target="tpu_custom_call" | custom-call | flops 6000000000 | bytes 6291456 | tf_op jit(solution)/shard_map/pallas_call | solution.py:395
  72.0 1.3 %copy.8 = bf16[2048,512]{1,0:T(8,128)(2,1)} copy(bf16[2048,512]{1,0:T(8,128)(2,1)S(1)} %bitcast.1) | data formatting | bytes 4194304

commit v6 on v4

--- a/solution.py
+++ b/solution.py
@@ -160,9 +160,8 @@
 
     kv_column(0)
     kv_row(0)
-    wz_copy(0).start()
     kv_column(1)
-    for part in range(1, 4):
+    for part in range(4):
         wz_copy(part).start()
     kv_relay(0)
     kv_row(1)

time: 73.4 us -> 73.4 us (level)
  no operation moved by 1% of the time
where the time goes in v6:
time: 73.4 us; the launch traced here: 73.3 us
  Pallas kernels  72 us (98%)
  local copies, waits for them, and re-layouts  1.32 us (2%)
    pallas_call x1, Pallas kernels, shards(): pl.pallas_call(kernel, out_shape=pltpu.VMEM((16, TOK, width), BF16), in_s...  72 us

profile of v6, /device:TPU:1, one launch (start us, length us, event | category | flops | bytes accessed | tf_op | source)
XLA Modules:
  0.0 73.3 jit_solution(8562752407153358269)
XLA Ops:
  0.0 72.0 %shard_map.64 = bf16[16,128,512]{2,1,0:T(8,128)(2,1)S(1)} custom-call(bf16[128,2048]{1,0:T(8,128)(2,1)} %q_hbm.1, bf16[128,256]{1,0:T(8,128)(2,1)} %k_hbm.1, bf16[128,256]{1,0:T(8,128)(2,1)} %v_hbm.1, bf16[2048,512]{1,0:T(8,128)(2,1)} %w_hbm.1, s32[1,16]{1,0:T(1,128)} %len_ref.1, s32[1,16]{1,0:T(1,128)} %dest_ref.1), custom_call_target="tpu_custom_call" | custom-call | flops 6000000000 | bytes 6291456 | tf_op jit(solution)/shard_map/pallas_call | solution.py:395
  72.0 1.3 %copy.8 = bf16[2048,512]{1,0:T(8,128)(2,1)} copy(bf16[2048,512]{1,0:T(8,128)(2,1)S(1)} %bitcast.1) | data formatting | bytes 4194304
